TPU v7x, 32 devices: a whole 2x2x4 slice. The times are simulated.
32 devices in a mesh: ctx: 8 (over y, x, core), head: 4 (over z).
Axes of the slice: x: 2, y: 2, z: 4, core: 2. Of those that a mesh axis runs over, the one named last changes fastest.
Arguments:
- queries: bfloat16 [1024, 12288], P('ctx', 'head'), may hold values from -8 to 8
- latents: bfloat16 [1024, 512], P('ctx'), may hold values from -4 to 4
- rope_key: bfloat16 [1024, 64], P('ctx'), may hold values from -8 to 8
- up_key_weight: bfloat16 [512, 8192], P(None, 'head'), may hold values from -0.5 to 0.5
- up_value_weight: bfloat16 [512, 8192], P(None, 'head'), may hold values from -0.25 to 0.25
- out_grad: bfloat16 [1024, 8192], P('ctx', 'head'), may hold values from -6 to 6
- group_order: int32 [16], replicated, may hold values from 0 to 15, as said below
Outputs:
- query_grad: bfloat16 [1024, 12288], P('ctx', 'head')
- latent_grad: float32 [1024, 512], P('ctx')
- rope_grad: float32 [1024, 64], P('ctx')
- up_key_grad: float32 [512, 8192], P('ctx', 'head')
- up_value_grad: float32 [512, 8192], P('ctx', 'head')
Inputs may be any that keep to these rules, and one draw needn't show every extreme that they name: A permutation of the 16 group numbers; storage slot k (rows k * 64 to k * 64 + 63) holds the sequence positions group_order[k] * 64 on, in order.
All inputs are finite; a program needn't handle non-finite values.
Results may differ from a plain program's by a relative error of at most 0.017.
Values may be sent and summed in bfloat16 or wider, within the bound.
A program may use at most 64 MiB of HBM per device.

v0:
```python
import jax
import jax.numpy as jnp
from jax import lax
from jax.sharding import PartitionSpec as P

D_LATENT = 512
ROPE = 64
NOPE = 128
VDIM = 128


NEG_FILL = -1e30


def product(pattern, left_side, right_side):
    return jnp.einsum(pattern, left_side, right_side, preferred_element_type=jnp.float32)


def token_positions(group_order, row_ids, group_len):
    slot_ids = row_ids // group_len
    slot_table = jnp.arange(group_order.shape[0], dtype=jnp.int32)
    picked = jnp.sum(
        jnp.where(slot_ids[:, None] == slot_table[None, :], group_order[None, :], 0), axis=1
    )
    return picked * group_len + row_ids % group_len


def per_device(queries, latents, rope_key, up_key_weight, up_value_weight, out_grad, group_order):
    tok_count = queries.shape[0]
    head_count = up_key_weight.shape[1] // NOPE
    group_len = tok_count // 2
    scale_factor = (NOPE + ROPE) ** (-0.5)
    shaped = queries.reshape(tok_count, head_count, NOPE + ROPE)
    query_nope = shaped[:, :, :NOPE]
    query_rope = shaped[:, :, NOPE:]
    up_key = up_key_weight.reshape(D_LATENT, head_count, NOPE)
    up_value = up_value_weight.reshape(D_LATENT, head_count, VDIM)
    grad_out = out_grad.reshape(tok_count, head_count, VDIM)
    query_abs = product("thd,khd->thk", query_nope, up_key).astype(jnp.bfloat16)
    grad_lat = product("thd,khd->thk", grad_out, up_value).astype(jnp.bfloat16)
    own_rows = lax.axis_index("ctx") * tok_count + jnp.arange(tok_count, dtype=jnp.int32)
    query_pos = token_positions(group_order, own_rows, group_len)

    def piece_scores(latent_piece, rope_piece):
        scores = product("thk,nk->thn", query_abs, latent_piece) + product(
            "thr,nr->thn", query_rope, rope_piece
        )
        return scores * scale_factor

    latent_piece = lax.all_gather(latents, "ctx", axis=0, tiled=True)
    rope_piece = lax.all_gather(rope_key, "ctx", axis=0, tiled=True)
    row_count = latent_piece.shape[0]
    key_pos = token_positions(group_order, jnp.arange(row_count, dtype=jnp.int32), group_len)
    visible = key_pos[None, None, :] <= query_pos[:, None, None]
    run_max = jnp.full((tok_count, head_count), NEG_FILL, jnp.float32)
    scores = piece_scores(latent_piece, rope_piece)
    grad_prob = product("thk,nk->thn", grad_lat, latent_piece)
    new_max = jnp.maximum(run_max, jnp.max(jnp.where(visible, scores, NEG_FILL), axis=2))
    weights = jnp.where(visible, jnp.exp(scores - new_max[:, :, None]), 0.0)
    forward_state = (new_max, jnp.sum(weights, axis=2), jnp.sum(weights * grad_prob, axis=2))
    run_max, run_sum, run_dot = forward_state
    log_total = run_max + jnp.log(run_sum)
    row_delta = run_dot / run_sum
    latent_piece = lax.all_gather(latents, "ctx", axis=0, tiled=True)
    rope_piece = lax.all_gather(rope_key, "ctx", axis=0, tiled=True)
    row_count = latent_piece.shape[0]
    key_pos = token_positions(group_order, jnp.arange(row_count, dtype=jnp.int32), group_len)
    visible = key_pos[None, None, :] <= query_pos[:, None, None]
    scores = piece_scores(latent_piece, rope_piece)
    softmax_rows = jnp.where(visible, jnp.exp(scores - log_total[:, :, None]), 0.0)
    grad_prob = product("thk,nk->thn", grad_lat, latent_piece)
    grad_score = softmax_rows * (grad_prob - row_delta[:, :, None]) * scale_factor
    probs_low = softmax_rows.astype(jnp.bfloat16)
    grad_low = grad_score.astype(jnp.bfloat16)
    acc_out = product("thn,nk->thk", probs_low, latent_piece)
    acc_query = product("thn,nk->thk", grad_low, latent_piece)
    acc_rope = product("thn,nr->thr", grad_low, rope_piece)
    latent_part = product("thn,thk->nk", grad_low, query_abs) + product(
        "thn,thk->nk", probs_low, grad_lat
    )
    rope_part = product("thn,thr->nr", grad_low, query_rope)
    all_latent = latent_part
    all_rope = rope_part
    backward_state = (acc_query, acc_rope, acc_out, all_latent, all_rope)
    acc_query, acc_rope, acc_out, all_latent, all_rope = backward_state
    grad_abs = acc_query.astype(jnp.bfloat16)
    grad_nope = product("thk,khd->thd", grad_abs, up_key)
    query_grad = (
        jnp.concatenate([grad_nope, acc_rope], axis=2).astype(jnp.bfloat16).reshape(tok_count, -1)
    )
    out_low = acc_out.astype(jnp.bfloat16)
    weight_key_grad = product("thk,thd->khd", grad_abs, query_nope).reshape(D_LATENT, -1)
    weight_value_grad = product("thk,thd->khd", out_low, grad_out).reshape(D_LATENT, -1)
    up_key_grad, up_value_grad = (
        lax.psum_scatter(
            weight_key_grad.astype(jnp.bfloat16), "ctx", scatter_dimension=0, tiled=True
        ).astype(jnp.float32),
        lax.psum_scatter(
            weight_value_grad.astype(jnp.bfloat16), "ctx", scatter_dimension=0, tiled=True
        ).astype(jnp.float32),
    )
    partial_latent, partial_rope = (
        lax.psum_scatter(
            all_latent.astype(jnp.bfloat16), "ctx", scatter_dimension=0, tiled=True
        ).astype(jnp.float32),
        lax.psum_scatter(
            all_rope.astype(jnp.bfloat16), "ctx", scatter_dimension=0, tiled=True
        ).astype(jnp.float32),
    )
    latent_grad, rope_grad = (
        lax.psum(partial_latent.astype(jnp.bfloat16), "head").astype(jnp.float32),
        lax.psum(partial_rope.astype(jnp.bfloat16), "head").astype(jnp.float32),
    )
    return (query_grad, latent_grad, rope_grad, up_key_grad, up_value_grad)


def solution(mesh):
    placed = (
        P("ctx", "head"),
        P("ctx", None),
        P("ctx", None),
        P(None, "head"),
        P(None, "head"),
        P("ctx", "head"),
        P(),
    )
    return jax.shard_map(
        per_device,
        mesh=mesh,
        in_specs=placed,
        out_specs=(
            P("ctx", "head"),
            P("ctx", None),
            P("ctx", None),
            P("ctx", "head"),
            P("ctx", "head"),
        ),
        check_vma=False,
    )
```

profile of v0, /device:TPU:0, one launch (start us, length us, event | category | flops | bytes accessed | tf_op | source)
XLA Modules:
  0.0 266.9 jit_solution(16135613890556101649)
XLA Ops:
  7.2 0.0 copy-start
  7.2 0.0 copy-start.10
  7.2 0.0 copy-start.11
  7.2 0.0 all-gather.2.cloned.1.call-start
  7.2 0.7 all-gather.2.cloned.1.call-update
  7.9 0.0 reduce-scatter.7.cloned.1.call-start
  8.0 1.3 copy.91
  9.3 1.5 copy.63
  10.8 3.9 %copy.90 = bf16[512,2048]{0,1:T(8,128)(2,1)} copy(bf16[512,2048]{1,0:T(8,128)(2,1)} %param.10) | data formatting | bytes 4194304 | tf_op jit(solution)/shard_map/reshape | solution.py:36
  14.7 0.0 copy-done.10
  14.7 11.7 %all_gather.9 = bf16[1024,64]{0,1:T(8,128)(2,1)} all-gather(bf16[128,64]{0,1:T(8,128)(2,1)S(1)} %copy-done.10), channel_id=1, replica_groups=mesh['ctx'=8,'head'=4] {'ctx'}, dimensions={0}, use_global_device_ids=true | all-gather | bytes 147456 | tf_op jit(solution)/shard_map/all_gather | solution.py:65
  26.5 0.0 copy-done.11
  26.5 0.1 select_reduce_fusion.2
  26.6 0.1 select_reduce_fusion.1
  26.7 0.1 broadcast_compare_fusion
  26.9 0.0 copy-done
  26.9 2.1 fusion.21
  28.9 2.1 convolution_convert_fusion.2
  31.1 5.3 %all-gather.2.cloned.1.call-done = bf16[1024,512]{1,0:T(8,128)(2,1)} async-done(((bf16[128,512]{1,0:T(8,128)(2,1)}), bf16[1024,512]{1,0:T(8,128)(2,1)}) %all-gather.2.cloned.1.call-update) | async-done | bytes 1048592 | tf_op jit(solution)/shard_map/all_gather | solution.py:64
  36.4 4.3 %fusion.12 = f32[128,16,1024]{2,0,1:T(8,128)S(1)} fusion(bf16[16,512,128]{2,1,0:T(8,128)(2,1)} %convolution_convert_fusion.2, bf16[1024,512]{1,0:T(8,128)(2,1)} %all-gather.2.cloned.1.call-done), kind=kOutput, calls=%fused_computation.19 | convolution fusion | flops 2147483648 | bytes 11534336 | tf_op jit(solution)/shard_map/thk,nk->thn/dot_general | solution.py:16
  40.7 2.1 select_reduce_fusion
  42.9 4.7 %fusion = (f32[128,16]{0,1:T(8,128)S(1)}, f32[128,16]{0,1:T(8,128)S(1)}, f32[128,16,1024]{2,0,1:T(8,128)S(1)}) fusion(f32[128,16,1024]{2,0,1:T(8,128)S(1)} %get-tuple-element.30, f32[128,16]{0,1:T(8,128)S(1)} %broadcast_maximum_fusion, pred[128,1024]{1,0:T(8,128)(4,1)S(1)} %broadcast_compare_fusion, bf16[1024,512]{1,0:T(8,128)(2,1)S(1)} %copy-done.12, ...), kind=kOutput, calls=%fused_computation.6 | convolution fusion | flops 2157965312 | bytes 20078592 | tf_op jit(solution)/shard_map/thk,nk->thn/dot_general | solution.py:16
  47.6 3.2 %fusion.6 = f32[1024,512,1]{1,0,2:T(8,128)S(1)} fusion(bf16[16,512,128]{2,1,0:T(8,128)(2,1)S(1)} %copy-done.7, f32[128,16,1024]{2,0,1:T(8,128)S(1)} %get-tuple-element.30, f32[128,16]{0,1:T(8,128)S(1)} %get-tuple-element.27, pred[128,1024]{1,0:T(8,128)(4,1)S(1)} %broadcast_compare_fusion), kind=kOutput, calls=%fused_computation.13 | convolution fusion | flops 2153775104 | bytes 12722176 | tf_op jit(solution)/shard_map/thn,thk->nk/dot_general | solution.py:16
  50.8 0.0 copy-done.2
  50.8 0.0 copy-start.6
  50.8 3.1 %multiply_convert_fusion = bf16[128,16,1024]{2,0,1:T(8,128)(2,1)S(1)} fusion(f32[128,16,1024]{2,0,1:T(8,128)S(1)} %get-tuple-element.31, f32[128,16,1024]{2,0,1:T(8,128)S(1)} %get-tuple-element.30, f32[128,16]{0,1:T(8,128)S(1)} %get-tuple-element.28, f32[128,16]{0,1:T(8,128)S(1)} %get-tuple-element.27, pred[128,1024]{1,0:T(8,128)(4,1)S(1)} %broadcast_compare_fusion), kind=kLoop, calls=%fused_computation | loop fusion | flops 12582912 | bytes 21118976 | tf_op jit(solution)/shard_map/convert_element_type | solution.py:74
  53.9 1.9 copy-done.1
  55.9 0.0 copy-done.6
  55.9 3.4 %fusion.5 = bf16[1024,512]{1,0:T(8,128)(2,1)} fusion(f32[1024,512,1]{1,0,2:T(8,128)S(1)} %fusion.6, bf16[128,16,1024]{2,0,1:T(8,128)(2,1)S(1)} %multiply_convert_fusion, bf16[16,512,128]{2,1,0:T(8,128)(2,1)S(1)} %copy-done.6), kind=kOutput, calls=%fused_computation.12 | convolution fusion | flops 2148532224 | bytes 9437184 | tf_op jit(solution)/shard_map/thn,thk->nk/dot_general | solution.py:16
  59.3 0.0 reduce-scatter.7.cloned.1.call-update
  59.3 0.0 reduce-scatter.13.cloned.1.call-start
  59.3 3.7 %fusion.27 = bf16[1024,64]{0,1:T(8,128)(2,1)} fusion(bf16[128,16,1024]{2,0,1:T(8,128)(2,1)} %copy-done.1, bf16[128,16,192]{0,2,1:T(8,128)(2,1)S(1)} %bitcast.80), kind=kOutput, calls=%fused_computation.33 | convolution fusion | flops 268500992 | bytes 4587520 | tf_op jit(solution)/shard_map/thn,thr->nr/dot_general | solution.py:16
  63.0 1.7 copy.87
  64.8 0.0 reduce-scatter.13.cloned.1.call-update
  64.8 0.0 all-reduce.2.cloned.1.call-start
  64.8 6.3 %convolution_convert_fusion = bf16[128,16,512]{2,0,1:T(8,128)(2,1)} fusion(bf16[128,16,1024]{2,0,1:T(8,128)(2,1)} %copy-done.1, bf16[1024,512]{1,0:T(8,128)(2,1)} %all-gather.2.cloned.1.call-done), kind=kOutput, calls=%fused_computation.24 | convolution fusion | flops 2148532224 | bytes 7340032 | tf_op jit(solution)/shard_map/thn,nk->thk/dot_general | solution.py:16
  71.1 24.4 %reduce-scatter.7.cloned.1.call-done = bf16[128,512]{1,0:T(8,128)(2,1)} async-done(((bf16[1024,512]{1,0:T(8,128)(2,1)}), bf16[128,512]{1,0:T(8,128)(2,1)}) %reduce-scatter.7.cloned.1.call-update) | async-done | bytes 131088 | tf_op jit(solution)/shard_map/reduce_scatter | solution.py:103
  95.5 0.0 all-reduce.2.cloned.1.call-update
  95.5 0.0 reduce-scatter.9.cloned.1.call-start
  95.5 3.6 %convolution_convert_fusion.1 = bf16[16,512,128]{1,2,0:T(8,128)(2,1)} fusion(bf16[128,16,512]{2,0,1:T(8,128)(2,1)} %convolution_convert_fusion, bf16[128,16,192]{0,2,1:T(8,128)(2,1)S(1)} %bitcast.81), kind=kOutput, calls=%fused_computation.27 | convolution fusion | flops 269484032 | bytes 4718592 | tf_op jit(solution)/shard_map/thk,thd->khd/dot_general | solution.py:16
  99.1 3.9 %copy.76 = bf16[512,2048]{1,0:T(8,128)(2,1)} copy(bf16[512,2048]{0,1:T(8,128)(2,1)} %bitcast.77) | data formatting | bytes 4194304 | tf_op jit(solution)/shard_map/convert_element_type | solution.py:96
  103.1 0.0 reduce-scatter.9.cloned.1.call-update
  103.1 0.3 reduce-scatter.11.cloned.1.call-start
  103.4 8.1 %fusion.18 = bf16[16,512,128]{1,2,0:T(8,128)(2,1)} fusion(bf16[128,16,128]{0,2,1:T(8,128)(2,1)S(1)} %bitcast.84, bf16[1024,512]{1,0:T(8,128)(2,1)} %all-gather.2.cloned.1.call-done, f32[128,16,1024]{2,0,1:T(8,128)} %copy-done.2, f32[128,16]{0,1:T(8,128)S(1)} %get-tuple-element.27, pred[128,1024]{1,0:T(8,128)(4,1)S(1)} %broadcast_compare_fusion), kind=kOutput, calls=%fused_computation.25 | convolution fusion | flops 2424307712 | bytes 12197888 | tf_op jit(solution)/shard_map/thk,thd->khd/dot_general | solution.py:16
  111.5 4.0 %copy.78 = bf16[512,2048]{1,0:T(8,128)(2,1)} copy(bf16[512,2048]{0,1:T(8,128)(2,1)} %bitcast.85) | data formatting | bytes 4194304 | tf_op jit(solution)/shard_map/convert_element_type | solution.py:99
  115.5 0.0 reduce-scatter.11.cloned.1.call-update
  115.5 0.0 copy-done.9
  115.5 0.0 copy-start.4
  115.5 0.0 copy-start.5
  115.5 3.7 %convolution_convert_fusion.4 = bf16[128,16,64]{0,2,1:T(8,128)(2,1)S(1)} fusion(bf16[128,16,1024]{2,0,1:T(8,128)(2,1)} %copy-done.1, bf16[1024,64]{0,1:T(8,128)(2,1)S(1)} %copy-done.9), kind=kOutput, calls=%fused_computation.31 | convolution fusion | flops 268566528 | bytes 4587520 | tf_op jit(solution)/shard_map/thn,nr->thr/dot_general | solution.py:16
  119.3 0.0 copy-done.4
  119.3 0.7 fusion.26
  120.0 0.1 pad_maximum_fusion
  120.1 1.2 copy.79
  121.2 11.4 %reduce-scatter.13.cloned.1.call-done = bf16[128,64]{1,0:T(8,128)(2,1)} async-done(((bf16[1024,64]{1,0:T(8,128)(2,1)}), bf16[128,64]{1,0:T(8,128)(2,1)}) %reduce-scatter.13.cloned.1.call-update) | async-done | bytes 16400
  132.7 0.8 copy.88
  133.5 18.8 %psum.15 = bf16[128,64]{0,1:T(8,128)(2,1)S(1)} all-reduce(bf16[128,64]{0,1:T(8,128)(2,1)S(1)} %copy.88), channel_id=1, replica_groups=mesh['ctx'=8,'head'=4] {'head'}, use_global_device_ids=true, to_apply=%region_8.9 | all-reduce | flops 8192 | bytes 32768 | tf_op jit(solution)/shard_map/psum | solution.py:112
  152.3 0.6 convert_element_type.80
  152.9 16.5 %all-reduce.2.cloned.1.call-done = bf16[128,512]{1,0:T(8,128)(2,1)} async-done(((bf16[128,512]{1,0:T(8,128)(2,1)}), bf16[128,512]{1,0:T(8,128)(2,1)}) %all-reduce.2.cloned.1.call-update) | async-done | bytes 131088 | tf_op jit(solution)/shard_map/psum | solution.py:111
  169.4 1.6 convert_element_type.78
  171.1 42.4 %reduce-scatter.9.cloned.1.call-done = bf16[64,2048]{1,0:T(8,128)(2,1)} async-done(((bf16[512,2048]{1,0:T(8,128)(2,1)}), bf16[64,2048]{1,0:T(8,128)(2,1)}) %reduce-scatter.9.cloned.1.call-update) | async-done | bytes 262160 | tf_op jit(solution)/shard_map/reduce_scatter | solution.py:95
  213.5 1.8 convert_element_type.84
  215.2 43.0 %reduce-scatter.11.cloned.1.call-done = bf16[64,2048]{1,0:T(8,128)(2,1)} async-done(((bf16[512,2048]{1,0:T(8,128)(2,1)}), bf16[64,2048]{1,0:T(8,128)(2,1)}) %reduce-scatter.11.cloned.1.call-update) | async-done | bytes 262160 | tf_op jit(solution)/shard_map/reduce_scatter | solution.py:98
  258.2 1.8 convert_element_type.89
  (18 shorter events, 0.1 us)
Async XLA Ops:
  7.2 19.7 %copy-start = (bf16[512,2048]{1,0:T(8,128)(2,1)S(1)}, bf16[512,2048]{1,0:T(8,128)(2,1)}, u32[]{:S(2)}) copy-start(bf16[512,2048]{1,0:T(8,128)(2,1)} %param.11) | copy-start | bytes 6291460
  7.2 7.6 %copy-start.10 = (bf16[128,64]{0,1:T(8,128)(2,1)S(1)}, bf16[128,64]{0,1:T(8,128)(2,1)}, u32[]{:S(2)}) copy-start(bf16[128,64]{0,1:T(8,128)(2,1)} %param.9) | copy-start | bytes 49156
  7.2 19.3 %copy-start.11 = (s32[16]{0:T(128)S(1)}, s32[16]{0:T(128)}, u32[]{:S(2)}) copy-start(s32[16]{0:T(128)} %param.13) | copy-start | bytes 196
  7.2 29.2 %all-gather.2.cloned.1.call-start = ((), (), s32[]{:S(2)}) async-start(), calls=%async_computation.4 | async-start | bytes 1179648 | tf_op jit(solution)/shard_map/all_gather | solution.py:64
  7.9 87.5 %reduce-scatter.7.cloned.1.call-start = ((), (), s32[]{:S(2)}) async-start(), calls=%async_computation.5 | async-start | bytes 1179648 | tf_op jit(solution)/shard_map/reduce_scatter | solution.py:103
  14.7 14.2 %copy-start.3 = (bf16[512,2048]{0,1:T(8,128)(2,1)S(1)}, bf16[512,2048]{0,1:T(8,128)(2,1)}, u32[]{:S(2)}) copy-start(bf16[512,2048]{0,1:T(8,128)(2,1)} %copy.90) | copy-start | bytes 6291460
  36.4 4.3 %copy-start.8 = (bf16[1024,64]{0,1:T(8,128)(2,1)S(1)}, bf16[1024,64]{0,1:T(8,128)(2,1)}, u32[]{:S(2)}) copy-start(bf16[1024,64]{0,1:T(8,128)(2,1)} %all_gather.9) | copy-start | bytes 393220
  40.7 2.1 copy-start.7
  40.7 2.1 copy-start.12
  42.8 8.0 %copy-start.2 = (f32[128,16,1024]{2,0,1:T(8,128)}, f32[128,16,1024]{2,0,1:T(8,128)S(1)}, u32[]{:S(2)}) copy-start(f32[128,16,1024]{2,0,1:T(8,128)S(1)} %get-tuple-element.30) | copy-start | bytes 25165828
  50.8 5.1 %copy-start.6 = (bf16[16,512,128]{2,1,0:T(8,128)(2,1)S(1)}, bf16[16,512,128]{2,1,0:T(8,128)(2,1)}, u32[]{:S(2)}) copy-start(bf16[16,512,128]{2,1,0:T(8,128)(2,1)} %convolution_convert_fusion.2) | copy-start | bytes 6291460
  53.9 2.0 copy-start.1
  59.3 73.4 %reduce-scatter.13.cloned.1.call-start = ((), (), s32[]{:S(2)}) async-start(), calls=%async_computation.9 | async-start | bytes 294912
  64.8 104.6 %all-reduce.2.cloned.1.call-start = ((), (), s32[]{:S(2)}) async-start(), calls=%async_computation.6 | async-start | bytes 262144 | tf_op jit(solution)/shard_map/psum | solution.py:111
  95.5 118.0 %reduce-scatter.9.cloned.1.call-start = ((), (), s32[]{:S(2)}) async-start(), calls=%async_computation.7 | async-start | bytes 2359296 | tf_op jit(solution)/shard_map/reduce_scatter | solution.py:95
  103.1 155.1 %reduce-scatter.11.cloned.1.call-start = ((), (), s32[]{:S(2)}) async-start(), calls=%async_computation.8 | async-start | bytes 2359296 | tf_op jit(solution)/shard_map/reduce_scatter | solution.py:98
  111.5 4.0 %copy-start.9 = (bf16[1024,64]{0,1:T(8,128)(2,1)S(1)}, bf16[1024,64]{0,1:T(8,128)(2,1)}, u32[]{:S(2)}) copy-start(bf16[1024,64]{0,1:T(8,128)(2,1)} %all_gather.9) | copy-start | bytes 393220
  115.5 3.8 %copy-start.4 = (bf16[512,2048]{0,1:T(8,128)(2,1)S(1)}, bf16[512,2048]{0,1:T(8,128)(2,1)}, u32[]{:S(2)}) copy-start(bf16[512,2048]{0,1:T(8,128)(2,1)} %copy.90) | copy-start | bytes 6291460
  115.5 3.7 %copy-start.5 = (bf16[128,16,512]{2,0,1:T(8,128)(2,1)S(1)}, bf16[128,16,512]{2,0,1:T(8,128)(2,1)}, u32[]{:S(2)}) copy-start(bf16[128,16,512]{2,0,1:T(8,128)(2,1)} %convolution_convert_fusion) | copy-start | bytes 6291460
Sparse Core Ops, SparseCore 0:
  9.9 26.3 all-gather.1
  59.4 36.0 reduce-scatter.6
  99.1 33.5 reduce-scatter.12
  135.0 34.4 all-reduce.1
  172.6 40.8 reduce-scatter.8
  216.9 41.2 reduce-scatter.10
where the time goes:
time: 268 us; the launch traced here: 267 us
  waiting for transfers between devices  144 us (54%)
  matrix products  47.9 us (18%)
  blocking collectives  30.5 us (11%)
  local copies, waits for them, and re-layouts  20.4 us (8%)
  between operations  14.4 us (5%)
  other arithmetic  9.36 us (3%)
    dot_general x13, matrix products, product(): jnp.einsum(pattern, left_side, right_side, preferred_element_type=jnp.flo...  47.9 us
    reduce_scatter x1, waiting for transfers between devices, per_device(): lax.psum_scatter(weight_value_grad.astype(jnp.bfloat16), 'ctx', scatter_d...  43 us
    reduce_scatter x1, waiting for transfers between devices, per_device(): lax.psum_scatter(weight_key_grad.astype(jnp.bfloat16), 'ctx', scatter_dim...  42.4 us
    reduce_scatter x1, waiting for transfers between devices, per_device(): lax.psum_scatter(all_latent.astype(jnp.bfloat16), 'ctx', scatter_dimensio...  24.4 us
    psum x1, blocking collectives, per_device(): lax.psum(partial_rope.astype(jnp.bfloat16), 'head').astype(jnp.float32)  18.8 us
    psum x1, waiting for transfers between devices, per_device(): lax.psum(partial_latent.astype(jnp.bfloat16), 'head').astype(jnp.float32)  16.5 us
    unnamed x7, waiting for transfers between devices  12.2 us
    all_gather x1, blocking collectives, per_device(): rope_piece = lax.all_gather(rope_key, 'ctx', axis=0, tiled=True)  11.7 us
  transfers between devices with their start and end apart: 6, of which 6 were waited for; matrix products, arithmetic and copies ran while one was open for 20% of the time, Pallas kernels for 0%

commit v1 on v0

v1 whole, which is shorter than its diff:
```python
import functools

import jax
import jax.numpy as jnp
from jax import lax
from jax.experimental import pallas as pl
from jax.experimental.pallas import tpu as pltpu
from jax.sharding import PartitionSpec as P

D_LATENT = 512
ROPE = 64
NOPE = 128
VDIM = 128
WIDE = 640

NEG_FILL = -1e30
MESH = pl.DeviceIdType.MESH
F32 = jnp.float32
BF16 = jnp.bfloat16


def dot(a, b, ca=1, cb=0):
    return lax.dot_general(a, b, (((ca,), (cb,)), ((), ())), preferred_element_type=F32)


def kernel(
    n, nz, lat_ref, rope_ref, order_ref, q_hbm, kw_hbm, vw_hbm, go_hbm,
    qg_ref, lg_ref, rg_ref, kg_ref, vg_ref,
    q_in, kw, vw, go, kv, kvt, bias, nope_s, qgl, pd,
    wbuf, wsib, wsum, wrecv, lbuf, lsib, lsum, lrecv, zbuf, zrecv, zout,
    in_sem, g_send, g_recv, ws_send, ws_recv, wc_send, wc_recv,
    ls_send, ls_recv, lc_send, lc_recv, zr_send, zr_recv, zg_send, zg_recv,
):
    T = lat_ref.shape[0]
    N = n * T
    C = n // 2
    pairs = kw.shape[1] // (2 * NOPE)
    nb = D_LATENT // n
    G = order_ref.shape[0]
    glen = N // G
    R = T // nz
    scale = (NOPE + ROPE) ** -0.5

    me = lax.axis_index("ctx")
    z = lax.axis_index("head")
    core = lax.rem(me, 2)
    chip = me // 2
    other = 1 - core
    sibling = chip * 2 + other

    def peer(r):
        return lax.rem(chip + r, C) * 2 + core

    def ahead(r):
        return lax.rem(z + r, nz)

    loads = [
        pltpu.make_async_copy(src, dst, in_sem.at[i])
        for i, (src, dst) in enumerate(
            ((q_hbm, q_in), (kw_hbm, kw), (go_hbm, go), (vw_hbm, vw))
        )
    ]
    for load in loads:
        load.start()

    barrier = pltpu.get_barrier_semaphore()
    pl.semaphore_signal(barrier, inc=1, device_id={"ctx": sibling}, device_id_type=MESH)
    for r in range(1, C):
        pl.semaphore_signal(barrier, inc=1, device_id={"ctx": peer(r)}, device_id_type=MESH)
    for r in range(1, nz):
        pl.semaphore_signal(barrier, inc=1, device_id={"head": ahead(r)}, device_id_type=MESH)

    own = pl.ds(pl.multiple_of(me * T, T), T)
    kv[own, :D_LATENT] = lat_ref[...]
    kv[own, D_LATENT:] = jnp.concatenate([rope_ref[...], jnp.zeros((T, WIDE - D_LATENT - ROPE), BF16)], axis=1)
    pl.semaphore_wait(barrier, 1 + (C - 1) + (nz - 1))

    def send(src, dst, s_sem, r_sem, where):
        return pltpu.make_async_remote_copy(
            src_ref=src, dst_ref=dst, send_sem=s_sem, recv_sem=r_sem,
            device_id=where, device_id_type=MESH,
        )

    gathers = []
    for r in range(1, C):
        cp = send(kv.at[own], kv.at[own], g_send.at[r], g_recv.at[r], {"ctx": peer(r)})
        cp.start()
        gathers.append(cp)
    to_sib = send(kv.at[own], kv.at[own], g_send.at[0], g_recv.at[0], {"ctx": sibling})
    to_sib.start()

    lane = lax.broadcasted_iota(jnp.int32, (1, T), 1)
    qpos = jnp.zeros((1, T), jnp.int32)
    for k in range(T // glen):
        base = order_ref[me * (T // glen) + k] * glen - k * glen
        qpos = jnp.where(lane // glen == k, base + lane, qpos)
    row = lax.broadcasted_iota(jnp.int32, (glen, T), 0)

    def fill_bias(g, carry):
        kpos = order_ref[g] * glen + row
        bias[pl.ds(pl.multiple_of(g * glen, glen), glen), :] = jnp.where(kpos <= qpos, 0.0, NEG_FILL)
        return carry

    lax.fori_loop(0, G, fill_bias, 0)
    for load in loads:
        load.wait()

    def prepare(p, carry):
        x = q_in[:, pl.ds(pl.multiple_of(p * 384, 128), 384)].astype(F32)
        for hh in range(2):
            cols = pl.ds(pl.multiple_of(p * 256 + hh * 128, 128), 128)
            nope = x[:, hh * 192:hh * 192 + 128].astype(BF16)
            rp = x[:, hh * 192 + 128:hh * 192 + 192]
            nope_s[p, hh * T:(hh + 1) * T, :] = nope
            top = pl.ds(pl.multiple_of(p * 4 * T + hh * T, T), T)
            low = pl.ds(pl.multiple_of(p * 4 * T + (2 + hh) * T, T), T)
            qgl[top, :D_LATENT] = dot(nope, kw[:, cols], 1, 1).astype(BF16)
            qgl[top, D_LATENT:] = jnp.concatenate([rp, jnp.zeros((T, 64), F32)], axis=1).astype(BF16)
            qgl[low, :D_LATENT] = dot(go[:, cols], vw[:, cols], 1, 1).astype(BF16)
            qgl[low, D_LATENT:] = jnp.zeros((T, WIDE - D_LATENT), BF16)
        return carry

    lax.fori_loop(0, pairs, prepare, 0)

    forwards = []
    for r in range(1, C):
        gathers[r - 1].wait_recv()
        block = lax.rem(chip - r + C, C) * 2 + core
        rows = pl.ds(pl.multiple_of(block * T, T), T)
        cp = send(kv.at[rows], kv.at[rows], g_send.at[C - 1 + r], g_recv.at[C - 1 + r], {"ctx": sibling})
        cp.start()
        forwards.append(cp)
    to_sib.wait_recv()
    for cp in forwards:
        cp.wait_recv()

    def flip(b, carry):
        rows = pl.ds(pl.multiple_of(b * T, T), T)
        kvt[:, rows] = kv[rows, :].T
        return carry

    lax.fori_loop(0, n, flip, 0)

    def w_sib(p):
        return send(wbuf.at[p, other], wsib.at[p], ws_send.at[p], ws_recv.at[p], {"ctx": sibling})

    def w_chip(p, r):
        to = lax.rem(chip + r, C)
        rows = pl.ds(pl.multiple_of(to * nb, nb), nb)
        return send(
            wsum.at[p, rows], wrecv.at[p, r - 1],
            wc_send.at[p, r - 1], wc_recv.at[p, r - 1], {"ctx": to * 2 + core},
        )

    def w_pass(p):
        w_sib(p).wait_recv()
        wsum[p] = (wbuf[p, core].astype(F32) + wsib[p].astype(F32)).astype(BF16)
        for r in range(1, C):
            w_chip(p, r).start()

    def pair(p, carry):
        q = qgl[pl.ds(pl.multiple_of(p * 4 * T, T), 2 * T), :]
        gl = qgl[pl.ds(pl.multiple_of(p * 4 * T + 2 * T, T), 2 * T), :D_LATENT]
        b1 = bias[...]
        s = dot(kv[...], q, 1, 1) * scale + jnp.concatenate([b1, b1], axis=1)
        g = dot(kv[:, :D_LATENT], gl, 1, 1)
        top = jnp.max(s, axis=0, keepdims=True)
        e = jnp.exp(s - top)
        inv = 1.0 / jnp.sum(e, axis=0, keepdims=True)
        delta = jnp.sum(e * g, axis=0, keepdims=True) * inv
        pr = e * inv
        ds = (pr * (g - delta) * scale).astype(BF16)
        pr = pr.astype(BF16)
        base = p * 4 * T
        pd[:, pl.ds(pl.multiple_of(base, T), 2 * T)] = ds
        pd[:, pl.ds(pl.multiple_of(base + 2 * T, T), 2 * T)] = pr
        got = dot(kvt[...], ds)
        ga = got[:D_LATENT].astype(BF16)
        ol = dot(kvt[:D_LATENT, :], pr).astype(BF16)
        rg = got[D_LATENT:].T
        parts = []
        for hh in range(2):
            cols = pl.ds(pl.multiple_of(p * 256 + hh * 128, 128), 128)
            gah = ga[:, hh * T:(hh + 1) * T]
            wk = dot(gah, nope_s[p, hh * T:(hh + 1) * T, :]).astype(BF16)
            wv = dot(ol[:, hh * T:(hh + 1) * T], go[:, cols]).astype(BF16)
            for c in range(C):
                for j in range(2):
                    d = 2 * c + j
                    wbuf[p, j, c * nb:(c + 1) * nb, hh * 128:(hh + 1) * 128] = wk[d * nb:(d + 1) * nb]
                    wbuf[p, j, c * nb:(c + 1) * nb, 256 + hh * 128:256 + (hh + 1) * 128] = wv[d * nb:(d + 1) * nb]
            parts.append((gah, cols))
        w_sib(p).start()
        pieces = []
        for hh, (gah, cols) in enumerate(parts):
            pieces.append(dot(gah, kw[:, cols], 0, 0))
            pieces.append(rg[hh * T:(hh + 1) * T, :ROPE])
        qg_ref[:, pl.ds(pl.multiple_of(p * 384, 128), 384)] = jnp.concatenate(pieces, axis=1).astype(BF16)

        @pl.when(p >= 1)
        def _():
            w_pass(p - 1)

        return carry

    lax.fori_loop(0, pairs, pair, 0)

    def l_sib(i):
        return send(lbuf.at[i, other], lsib.at[i], ls_send.at[i], ls_recv.at[i], {"ctx": sibling})

    def l_chip(i):
        to = lax.rem(chip + 1 + i, C) * 2 + core
        return send(lsum.at[i], lrecv.at[i], lc_send.at[i], lc_recv.at[i], {"ctx": to})

    def l_pass(i):
        l_sib(i).wait_recv()
        lsum[i] = (lbuf[i, core].astype(F32) + lsib[i].astype(F32)).astype(BF16)
        l_chip(i).start()

    def keys(i, carry):
        to = lax.rem(chip + 1 + i, C)
        part = dot(pd[pl.ds(pl.multiple_of(to * 2 * T, 2 * T), 2 * T), :], qgl[...]).astype(BF16)
        lbuf[i, 0] = part[:T]
        lbuf[i, 1] = part[T:]
        l_sib(i).start()

        @pl.when(i == 0)
        def _():
            w_pass(pairs - 1)

        @pl.when(i >= 1)
        def _():
            l_pass(i - 1)

        return carry

    lax.fori_loop(0, C, keys, 0)

    l_sib(C - 1).wait_recv()
    total = lbuf[C - 1, core].astype(F32) + lsib[C - 1].astype(F32)
    for i in range(C - 1):
        l_chip(i).wait_recv()
        total = total + lrecv[i].astype(F32)
    zbuf[...] = total.astype(BF16)

    def z_add(r):
        rows = pl.ds(pl.multiple_of(ahead(r) * R, R), R)
        return send(zbuf.at[rows], zrecv.at[r - 1], zr_send.at[r - 1], zr_recv.at[r - 1], {"head": ahead(r)})

    for r in range(1, nz):
        z_add(r).start()

    def w_end(p, carry):
        rows = pl.ds(pl.multiple_of(chip * nb, nb), nb)
        acc = wsum[p, rows, :].astype(F32)
        for r in range(1, C):
            w_chip(p, r).wait_recv()
            acc = acc + wrecv[p, r - 1].astype(F32)
        cols = pl.ds(pl.multiple_of(p * 256, 256), 256)
        kg_ref[:, cols] = acc[:, :256]
        vg_ref[:, cols] = acc[:, 256:]
        return carry

    lax.fori_loop(0, pairs - 1, w_end, 0)

    mine = pl.ds(pl.multiple_of(z * R, R), R)
    acc = zbuf[mine, :].astype(F32)
    for r in range(1, nz):
        z_add(r).wait_recv()
        acc = acc + zrecv[r - 1].astype(F32)
    zout[mine, :] = acc.astype(BF16)

    def z_all(r):
        return send(zout.at[mine], zout.at[mine], zg_send.at[r - 1], zg_recv.at[r - 1], {"head": ahead(r)})

    for r in range(1, nz):
        z_all(r).start()
    w_end(pairs - 1, 0)

    for cp in gathers + forwards + [to_sib]:
        cp.wait_send()

    def w_sent(p, carry):
        w_sib(p).wait_send()
        for r in range(1, C):
            w_chip(p, r).wait_send()
        return carry

    lax.fori_loop(0, pairs, w_sent, 0)
    for i in range(C):
        l_sib(i).wait_send()
        if i < C - 1:
            l_chip(i).wait_send()
    for r in range(1, nz):
        z_add(r).wait_send()
        z_all(r).wait()
    lg_ref[...] = zout[:, :D_LATENT].astype(F32)
    rg_ref[...] = zout[:, D_LATENT:].astype(F32)[:, :ROPE]


def per_device(n, nz, queries, latents, rope_key, up_key_weight, up_value_weight, out_grad, group_order):
    T = queries.shape[0]
    width = up_key_weight.shape[1]
    N, C, pairs, nb, R = n * T, n // 2, width // 256, D_LATENT // n, T // nz
    vm = pl.BlockSpec(memory_space=pltpu.VMEM)
    hbm = pl.BlockSpec(memory_space=pl.ANY)
    dma = pltpu.SemaphoreType.DMA

    def buf(*shape, dtype=BF16):
        return pltpu.VMEM(shape, dtype)

    flops = 2 * 2 * pairs * T * N * (3 * WIDE + 3 * D_LATENT)
    return pl.pallas_call(
        functools.partial(kernel, n, nz),
        out_shape=(
            jax.ShapeDtypeStruct(queries.shape, BF16),
            jax.ShapeDtypeStruct((T, D_LATENT), F32),
            jax.ShapeDtypeStruct((T, ROPE), F32),
            jax.ShapeDtypeStruct((nb, width), F32),
            jax.ShapeDtypeStruct((nb, width), F32),
        ),
        in_specs=[vm, vm, pl.BlockSpec(memory_space=pltpu.SMEM), hbm, hbm, hbm, hbm],
        out_specs=(vm,) * 5,
        scratch_shapes=[
            buf(*queries.shape), buf(*up_key_weight.shape), buf(*up_value_weight.shape), buf(*out_grad.shape),
            buf(N, WIDE), buf(WIDE, N), buf(N, T, dtype=F32), buf(pairs, 2 * T, NOPE),
            buf(pairs * 4 * T, WIDE), buf(N, pairs * 4 * T),
            buf(pairs, 2, C * nb, 512), buf(pairs, C * nb, 512), buf(pairs, C * nb, 512),
            buf(pairs, C - 1, nb, 512),
            buf(C, 2, T, WIDE), buf(C, T, WIDE), buf(C - 1, T, WIDE), buf(C - 1, T, WIDE),
            buf(T, WIDE), buf(nz - 1, R, WIDE), buf(T, WIDE),
            dma((4,)), dma((2 * C - 1,)), dma((2 * C - 1,)),
            dma((pairs,)), dma((pairs,)), dma((pairs, C - 1)), dma((pairs, C - 1)),
            dma((C,)), dma((C,)), dma((C - 1,)), dma((C - 1,)),
            dma((nz - 1,)), dma((nz - 1,)), dma((nz - 1,)), dma((nz - 1,)),
        ],
        compiler_params=pltpu.CompilerParams(
            collective_id=0, has_side_effects=True, vmem_limit_bytes=60 * 1024 * 1024
        ),
        cost_estimate=pl.CostEstimate(flops=flops, bytes_accessed=8 * 1024 * 1024, transcendentals=2 * pairs * T * N),
        name="mla_backward",
    )(latents, rope_key, group_order, queries, up_key_weight, up_value_weight, out_grad)


def solution(mesh):
    placed = (
        P("ctx", "head"),
        P("ctx", None),
        P("ctx", None),
        P(None, "head"),
        P(None, "head"),
        P("ctx", "head"),
        P(),
    )
    return jax.shard_map(
        functools.partial(per_device, mesh.shape["ctx"], mesh.shape["head"]),
        mesh=mesh,
        in_specs=placed,
        out_specs=(
            P("ctx", "head"),
            P("ctx", None),
            P("ctx", None),
            P("ctx", "head"),
            P("ctx", "head"),
        ),
        check_vma=False,
    )
```

time: 268 us -> 77.3 us (0.29)
  waiting for transfers between devices: 144 us -> 0 us
  Pallas kernels: 0 us -> 67.9 us
  matrix products: 47.9 us -> 0 us
  blocking collectives: 30.5 us -> 0 us
  between operations: 14.4 us -> 0.66 us
  local copies, waits for them, and re-layouts: 20.4 us -> 8.38 us
  other arithmetic: 9.36 us -> 0 us
    reduce_scatter x3 -> x0, waiting for transfers between devices: 110 us -> none  [the longest x1 43 us: per_device(): lax.psum_scatter(weight_value_grad.astype(jnp.bfloat16), 'ctx', scatter_d...]
    pallas_call x0 -> x1, Pallas kernels: none -> 67.9 us  [per_device(): pl.pallas_call(functools.partial(kernel, n, nz), out_shape=(jax.ShapeDtyp...]
    dot_general x13 -> x0, matrix products: 47.9 us -> none  [product(): jnp.einsum(pattern, left_side, right_side, preferred_element_type=jnp.flo...]
    psum x1 -> x0, blocking collectives: 18.8 us -> none  [per_device(): lax.psum(partial_rope.astype(jnp.bfloat16), 'head').astype(jnp.float32)]
    psum x1 -> x0, waiting for transfers between devices: 16.5 us -> none  [per_device(): lax.psum(partial_latent.astype(jnp.bfloat16), 'head').astype(jnp.float32)]
    unnamed x7 -> x0, waiting for transfers between devices: 12.2 us -> none
    all_gather x1 -> x0, blocking collectives: 11.7 us -> none  [per_device(): rope_piece = lax.all_gather(rope_key, 'ctx', axis=0, tiled=True)]
    convert_element_type x5 -> x0, other arithmetic: 8.94 us -> none  [the longest x2 3.55 us: per_device(): up_key_grad, up_value_grad = (lax.psum_scatter(weight_key_grad.astype(jnp...]
  transfers between devices with their start and end apart: 6 -> 0, of which waited for: 6 -> 0; matrix products, arithmetic and copies ran while one was open for 20% -> 0% of each run, Pallas kernels for 0% -> 0%
where the time goes in v1:
time: 77.3 us; the launch traced here: 77 us
  Pallas kernels  67.9 us (88%)
  local copies, waits for them, and re-layouts  8.38 us (11%)
    pallas_call x1, Pallas kernels, per_device(): pl.pallas_call(functools.partial(kernel, n, nz), out_shape=(jax.ShapeDtyp...  67.9 us
    unnamed x9, local copies, waits for them, and re-layouts  6.76 us
    pallas_call x1, local copies, waits for them, and re-layouts, per_device(): pl.pallas_call(functools.partial(kernel, n, nz), out_shape=(jax.ShapeDtyp...  1.62 us

profile of v1, /device:TPU:0, one launch (start us, length us, event | category | flops | bytes accessed | tf_op | source)
XLA Modules:
  0.0 77.0 jit_solution(11097292869486263322)
XLA Ops:
  0.6 1.4 %copy.12.rope_ref = bf16[128,64]{1,0:T(8,128)(2,1)} copy(bf16[128,64]{0,1:T(8,128)(2,1)} %param.9) | data formatting | bytes 32768 | tf_op args[2]
  2.1 67.9 %mla_backward.1 = (bf16[128,3072]{1,0:T(8,128)(2,1)}, f32[128,512]{1,0:T(8,128)}, f32[128,64]{1,0:T(8,128)}, f32[64,2048]{1,0:T(8,128)}, f32[64,2048]{1,0:T(8,128)}) custom-call(bf16[128,512]{1,0:T(8,128)(2,1)} %lat_ref.1, bf16[128,64]{1,0:T(8,128)(2,1)} %copy.12.rope_ref, s32[16]{0:T(128)} %order_ref.1, bf16[128,3072]{1,0:T(8,128)(2,1)} %q_hbm.1, ...), custom_call_target="tpu_custom_call" | custom-call | flops 14495514624 | bytes 8388608 | tf_op jit(solution)/shard_map/mla_backward/pallas_call | solution.py:313
  70.0 0.0 copy-start.1
  70.0 0.0 copy-start
  70.0 1.6 %copy.13 = f32[128,64]{0,1:T(8,128)} copy(f32[128,64]{1,0:T(8,128)} %get-tuple-element.7) | data formatting | bytes 65536 | tf_op jit(solution)/shard_map/mla_backward/pallas_call | solution.py:313
  71.6 2.1 %copy.18 = bf16[128,3072]{1,0:T(8,128)(2,1)} copy(bf16[128,3072]{1,0:T(8,128)(2,1)} %get-tuple-element.15) | data formatting | bytes 1572864
  73.7 1.7 %copy.19 = f32[128,512]{1,0:T(8,128)} copy(f32[128,512]{1,0:T(8,128)} %get-tuple-element.16) | data formatting | bytes 524288
  75.4 0.0 copy-done.1
  75.4 0.8 %copy.20 = f32[64,2048]{1,0:T(8,128)} copy(f32[64,2048]{1,0:T(8,128)S(1)} %copy-done.1) | data formatting | bytes 1048576
  76.2 0.0 copy-done
  76.2 0.8 %copy.21 = f32[64,2048]{1,0:T(8,128)} copy(f32[64,2048]{1,0:T(8,128)S(1)} %copy-done) | data formatting | bytes 1048576
Async XLA Ops:
  70.0 5.4 %copy-start.1 = (f32[64,2048]{1,0:T(8,128)S(1)}, f32[64,2048]{1,0:T(8,128)}, u32[]{:S(2)}) copy-start(f32[64,2048]{1,0:T(8,128)} %get-tuple-element.18) | copy-start | bytes 1572868
  70.0 6.2 %copy-start = (f32[64,2048]{1,0:T(8,128)S(1)}, f32[64,2048]{1,0:T(8,128)}, u32[]{:S(2)}) copy-start(f32[64,2048]{1,0:T(8,128)} %get-tuple-element.19) | copy-start | bytes 1572868

commit v2 on v1

--- a/solution.py
+++ b/solution.py
@@ -72,7 +72,9 @@
 
     own = pl.ds(pl.multiple_of(me * T, T), T)
     kv[own, :D_LATENT] = lat_ref[...]
-    kv[own, D_LATENT:] = jnp.concatenate([rope_ref[...], jnp.zeros((T, WIDE - D_LATENT - ROPE), BF16)], axis=1)
+    kv[own, D_LATENT:] = jnp.concatenate(
+        [rope_ref[...], jnp.zeros((WIDE - D_LATENT - ROPE, T), BF16)], axis=0
+    ).T
     pl.semaphore_wait(barrier, 1 + (C - 1) + (nz - 1))
 
     def send(src, dst, s_sem, r_sem, where):
@@ -122,6 +124,11 @@
 
     lax.fori_loop(0, pairs, prepare, 0)
 
+    def flip(b):
+        rows = pl.ds(pl.multiple_of(b * T, T), T)
+        kvt[:, rows] = kv[rows, :].T
+
+    flip(me)
     forwards = []
     for r in range(1, C):
         gathers[r - 1].wait_recv()
@@ -130,16 +137,12 @@
         cp = send(kv.at[rows], kv.at[rows], g_send.at[C - 1 + r], g_recv.at[C - 1 + r], {"ctx": sibling})
         cp.start()
         forwards.append(cp)
+        flip(block)
     to_sib.wait_recv()
-    for cp in forwards:
-        cp.wait_recv()
-
-    def flip(b, carry):
-        rows = pl.ds(pl.multiple_of(b * T, T), T)
-        kvt[:, rows] = kv[rows, :].T
-        return carry
-
-    lax.fori_loop(0, n, flip, 0)
+    flip(sibling)
+    for r in range(1, C):
+        forwards[r - 1].wait_recv()
+        flip(lax.rem(chip - r + C, C) * 2 + other)
 
     def w_sib(p):
         return send(wbuf.at[p, other], wsib.at[p], ws_send.at[p], ws_recv.at[p], {"ctx": sibling})
@@ -295,7 +298,20 @@
         z_add(r).wait_send()
         z_all(r).wait()
     lg_ref[...] = zout[:, :D_LATENT].astype(F32)
-    rg_ref[...] = zout[:, D_LATENT:].astype(F32)[:, :ROPE]
+    rg_ref[...] = zout[:, D_LATENT:].astype(F32).T[:ROPE]
+
+
+def hand_over(*refs):
+    src, dst, held, (into, out) = refs[:5], refs[5:10], refs[10:15], refs[15:]
+    reads = [pltpu.make_async_copy(src[i], held[i], into.at[i]) for i in range(5)]
+    writes = [pltpu.make_async_copy(held[i], dst[i], out.at[i]) for i in range(5)]
+    for cp in reads:
+        cp.start()
+    for read, write in zip(reads, writes):
+        read.wait()
+        write.start()
+    for cp in writes:
+        cp.wait()
 
 
 def per_device(n, nz, queries, latents, rope_key, up_key_weight, up_value_weight, out_grad, group_order):
@@ -310,12 +326,12 @@
         return pltpu.VMEM(shape, dtype)
 
     flops = 2 * 2 * pairs * T * N * (3 * WIDE + 3 * D_LATENT)
-    return pl.pallas_call(
+    results = pl.pallas_call(
         functools.partial(kernel, n, nz),
         out_shape=(
             jax.ShapeDtypeStruct(queries.shape, BF16),
             jax.ShapeDtypeStruct((T, D_LATENT), F32),
-            jax.ShapeDtypeStruct((T, ROPE), F32),
+            jax.ShapeDtypeStruct((ROPE, T), F32),
             jax.ShapeDtypeStruct((nb, width), F32),
             jax.ShapeDtypeStruct((nb, width), F32),
         ),
@@ -339,7 +355,16 @@
         ),
         cost_estimate=pl.CostEstimate(flops=flops, bytes_accessed=8 * 1024 * 1024, transcendentals=2 * pairs * T * N),
         name="mla_backward",
-    )(latents, rope_key, group_order, queries, up_key_weight, up_value_weight, out_grad)
+    )(latents, rope_key.T, group_order, queries, up_key_weight, up_value_weight, out_grad)
+    out = pl.pallas_call(
+        hand_over,
+        out_shape=tuple(jax.ShapeDtypeStruct(x.shape, x.dtype) for x in results),
+        in_specs=[hbm] * 5,
+        out_specs=(hbm,) * 5,
+        scratch_shapes=[pltpu.VMEM(x.shape, x.dtype) for x in results] + [dma((5,)), dma((5,))],
+        name="hand_over",
+    )(*results)
+    return (out[0], out[1], out[2].T, out[3], out[4])
 
 
 def solution(mesh):

time: 77.3 us -> 70.2 us (0.908)
  local copies, waits for them, and re-layouts: 8.38 us -> 0 us
  Pallas kernels: 67.9 us -> 69.4 us
    unnamed x9 -> x0, local copies, waits for them, and re-layouts: 6.76 us -> none
    pallas_call x0 -> x1, Pallas kernels: none -> 2.54 us  [per_device(): pl.pallas_call(hand_over, out_shape=tuple((jax.ShapeDtypeStruct(x.shape,...]
    pallas_call x1 -> x0, local copies, waits for them, and re-layouts: 1.62 us -> none  [per_device(): pl.pallas_call(functools.partial(kernel, n, nz), out_shape=(jax.ShapeDtyp...]
    pallas_call x1, Pallas kernels: 67.9 us -> 66.9 us  [per_device(): pl.pallas_call(functools.partial(kernel, n, nz), out_shape=(jax.ShapeDtyp...]
where the time goes in v2:
time: 70.2 us; the launch traced here: 70.1 us
  Pallas kernels  69.4 us (99%)
    pallas_call x1, Pallas kernels, per_device(): pl.pallas_call(functools.partial(kernel, n, nz), out_shape=(jax.ShapeDtyp...  66.9 us
    pallas_call x1, Pallas kernels, per_device(): pl.pallas_call(hand_over, out_shape=tuple((jax.ShapeDtypeStruct(x.shape,...  2.54 us

profile of v2, /device:TPU:0, one launch (start us, length us, event | category | flops | bytes accessed | tf_op | source)
XLA Modules:
  0.0 70.1 jit_solution(15621116768713756158)
XLA Ops:
  0.6 66.9 %mla_backward.1 = (bf16[128,3072]{1,0:T(8,128)(2,1)}, f32[128,512]{1,0:T(8,128)}, f32[64,128]{1,0:T(8,128)}, f32[64,2048]{1,0:T(8,128)}, f32[64,2048]{1,0:T(8,128)}) custom-call(bf16[128,512]{1,0:T(8,128)(2,1)} %lat_ref.1, bf16[64,128]{1,0:T(8,128)(2,1)} %bitcast.3, s32[16]{0:T(128)} %order_ref.1, bf16[128,3072]{1,0:T(8,128)(2,1)} %q_hbm.1, ...), custom_call_target="tpu_custom_call" | custom-call | flops 14495514624 | bytes 8388608 | tf_op jit(solution)/shard_map/mla_backward/pallas_call | solution.py:329
  67.5 2.5 %hand_over.1 = (bf16[128,3072]{1,0:T(8,128)(2,1)}, f32[128,512]{1,0:T(8,128)}, f32[64,128]{1,0:T(8,128)}, f32[64,2048]{1,0:T(8,128)}, f32[64,2048]{1,0:T(8,128)}) custom-call(bf16[128,3072]{1,0:T(8,128)(2,1)} %get-tuple-element.15.refs_0_, f32[128,512]{1,0:T(8,128)} %get-tuple-element.16.refs_1_, f32[64,128]{1,0:T(8,128)} %get-tuple-element.17.refs_2_, ...), custom_call_target="tpu_custom_call" | custom-call | tf_op jit(solution)/shard_map/hand_over/pallas_call | solution.py:359
